TPU v7x, 32 devices: a whole 2x2x4 slice. The times are simulated.
32 devices in a mesh: parts: 1, ctx: 4 (over z), pb: 4 (over y, x), row: 2 (over core).
Axes of the slice: x: 2, y: 2, z: 4, core: 2. Of those that a mesh axis runs over, the one named last changes fastest.
Arguments:
- queries: bfloat16 [2048, 3072], P(('parts', 'ctx', 'pb', 'row')), may hold values from -10 to 10
- cache_keys: bfloat16 [4096, 192], P(('parts', 'ctx')), may hold values from -10 to 10
- cache_values: bfloat16 [4096, 128], P(('parts', 'ctx')), may hold values from -6 to 6
- span_keys: bfloat16 [2048, 192], P(('parts', 'ctx')), may hold values from -10 to 10
- span_values: bfloat16 [2048, 128], P(('parts', 'ctx')), may hold values from -6 to 6
- pool_keys: float32 [32, 192], replicated, may hold values from 0.2 to 0.6
- pool_values: float32 [32, 128], replicated, may hold values from 0.05 to 0.3
- gate_logits: bfloat16 [2048, 48], P(('parts', 'ctx', 'pb', 'row')), may hold values from -6 to 6
- chosen_blocks: int32 [32, 16], P(('parts', 'ctx', 'pb', 'row')), may hold values from 0 to 95, as said below
- valid_counts: int32 [32], P(('parts', 'ctx', 'pb', 'row')), may hold values from 4 to 16
Outputs:
- mixed: bfloat16 [2048, 2048], P(('parts', 'ctx', 'pb', 'row'))
Inputs may be any that keep to these rules, and one draw needn't show every extreme that they name: `chosen_blocks`: slot 0 of tile t holds the tile's own block 64 + t. Slot s > 0 holds a block of the cache stored by ctx index (c + s) mod (4), where c is the ctx index that holds tile t; the blocks of one tile are distinct. Slots at or beyond the tile's valid count hold blocks too and are ignored.
All inputs are finite; a program needn't handle non-finite values.
Results may differ from a plain program's by a relative error of at most 0.0034.
The roundings to bfloat16 on the way count: a program that leaves them out, or rounds other values in their place, can miss the bound.
Values may be sent and summed in bfloat16 or wider, within the bound.
A program may use at most 64 MiB of HBM per device.

v0:
```python
import math
import jax
import jax.numpy as jnp
from jax import lax
from jax.sharding import PartitionSpec as P

HEADS = 16
CLEN = 32
STRIDE = 16
BLOCK = 64
WINDOW = 256
NEG_FILL = -1e30


def from_behind(value, axis, steps):
    count = lax.axis_size(axis)
    pairs = [(source, (source + steps) % count) for source in range(count)]
    return lax.ppermute(value, axis, pairs)


def pool_blocks(rows, extra, weights, stride):
    joined = jnp.concatenate([rows, extra], axis=0).astype(jnp.float32)
    blocks = rows.shape[0] // stride
    grouped = joined.reshape(blocks + 1, stride, rows.shape[1])
    leading = jnp.sum(grouped[:-1] * weights[None, :stride, :], axis=1)
    trailing = jnp.sum(grouped[1:] * weights[None, stride:, :], axis=1)
    return (leading + trailing).astype(jnp.bfloat16)


def attend(query_rows, keys, values, visible, score_scale):
    scores = jnp.dot(query_rows, keys.T, preferred_element_type=jnp.float32) * score_scale
    scores = jnp.where(visible, scores, NEG_FILL)
    highest = jnp.max(scores, axis=1, keepdims=True)
    exponent = jnp.where(visible, jnp.exp(scores - highest), 0.0)
    weights = exponent.astype(jnp.bfloat16)
    numerator = jnp.dot(weights, values, preferred_element_type=jnp.float32)
    return numerator / jnp.sum(exponent, axis=1, keepdims=True)


def local(
    queries,
    cache_keys,
    cache_values,
    span_keys,
    span_values,
    pool_keys,
    pool_values,
    gate_logits,
    chosen_blocks,
    valid_counts,
):
    owners = lax.axis_size("ctx")
    ctx_place = lax.axis_index("ctx")
    tile_place = lax.axis_index("pb") * lax.axis_size("row") + lax.axis_index("row")
    cache_len, key_width = cache_keys.shape
    value_width = cache_values.shape[1]
    span_len = span_keys.shape[0]
    tokens = queries.shape[0]
    tiles_here = chosen_blocks.shape[0]
    score_scale = 1.0 / math.sqrt(key_width)
    context_start = cache_len * owners
    local_start = tile_place * tokens
    first_pos = context_start + ctx_place * span_len + local_start
    row_count = tokens * HEADS
    query_rows = queries.reshape(row_count, key_width)
    row_pos = first_pos + jnp.arange(row_count, dtype=jnp.int32) // HEADS
    leader = ctx_place == 0
    outgoing = (
        jnp.where(leader, span_keys[:STRIDE], cache_keys[:STRIDE]),
        jnp.where(leader, span_values[:STRIDE], cache_values[:STRIDE]),
        span_keys[:STRIDE],
        span_values[:STRIDE],
    )
    heads_next = from_behind((outgoing[0], outgoing[1], outgoing[2], outgoing[3]), "ctx", -1)
    summary_keys = jnp.concatenate(
        [
            pool_blocks(cache_keys, heads_next[0], pool_keys, STRIDE),
            pool_blocks(span_keys, heads_next[2], pool_keys, STRIDE),
        ],
        axis=0,
    )
    summary_values = jnp.concatenate(
        [
            pool_blocks(cache_values, heads_next[1], pool_values, STRIDE),
            pool_blocks(span_values, heads_next[3], pool_values, STRIDE),
        ],
        axis=0,
    )
    cache_blocks = cache_len // STRIDE
    span_blocks = span_len // STRIDE
    per_ctx = cache_blocks + span_blocks
    first_row = jnp.int32(0)
    running_max = jnp.full((row_count,), NEG_FILL, jnp.float32)
    running_sum = jnp.zeros((row_count,), jnp.float32)
    running_out = jnp.zeros((row_count, value_width), jnp.float32)
    part_keys = lax.all_gather(summary_keys, "ctx", axis=0, tiled=True)
    part_values = lax.all_gather(summary_values, "ctx", axis=0, tiled=True)
    length = part_keys.shape[0]
    for lower_row in range(0, length, 512):
        upper_row = min(lower_row + 512, length)
        block_index = first_row + lower_row + jnp.arange(upper_row - lower_row, dtype=jnp.int32)
        owner_of = block_index // per_ctx
        within = block_index % per_ctx
        block_id = jnp.where(
            within < cache_blocks,
            owner_of * cache_blocks + within,
            owners * cache_blocks + owner_of * span_blocks + within - cache_blocks,
        )
        visible = (block_id * STRIDE + CLEN)[None, :] <= row_pos[:, None] + 1
        scores = (
            jnp.dot(
                query_rows, part_keys[lower_row:upper_row].T, preferred_element_type=jnp.float32
            )
            * score_scale
        )
        scores = jnp.where(visible, scores, NEG_FILL)
        new_max = jnp.maximum(running_max, jnp.max(scores, axis=1))
        exponent = jnp.where(visible, jnp.exp(scores - new_max[:, None]), 0.0)
        fading = jnp.exp(running_max - new_max)
        running_sum = running_sum * fading + jnp.sum(exponent, axis=1)
        running_out = running_out * fading[:, None] + jnp.dot(
            exponent.astype(jnp.bfloat16),
            part_values[lower_row:upper_row],
            preferred_element_type=jnp.float32,
        )
        running_max = new_max
    summary_out = running_out / running_sum[:, None]
    reach = chosen_blocks.shape[1] // owners
    arranged = chosen_blocks.reshape(tiles_here, reach, owners)
    column_of = (jnp.arange(owners, dtype=jnp.int32) - ctx_place) % owners
    requested = jnp.take(arranged, column_of, axis=2)
    wanted = lax.all_to_all(requested, "ctx", split_axis=2, concat_axis=2, tiled=True)
    cache_count = cache_len // BLOCK
    span_count = span_len // BLOCK
    from_cache = (wanted < owners * cache_count)[..., None, None]
    cache_slot = jnp.clip(wanted - ctx_place * cache_count, 0, cache_count - 1)
    span_slot = jnp.clip(wanted - owners * cache_count - ctx_place * span_count, 0, span_count - 1)
    served_keys = jnp.where(
        from_cache,
        cache_keys.reshape(cache_count, BLOCK, key_width)[cache_slot],
        span_keys.reshape(span_count, BLOCK, key_width)[span_slot],
    )
    served_values = jnp.where(
        from_cache,
        cache_values.reshape(cache_count, BLOCK, value_width)[cache_slot],
        span_values.reshape(span_count, BLOCK, value_width)[span_slot],
    )
    fetched_keys, fetched_values = (
        lax.all_to_all(served_keys, "ctx", split_axis=2, concat_axis=2, tiled=True),
        lax.all_to_all(served_values, "ctx", split_axis=2, concat_axis=2, tiled=True),
    )
    last_ctx = ctx_place == owners - 1
    tail_rows = from_behind(
        (
            jnp.where(last_ctx, cache_keys[-WINDOW:], span_keys[-WINDOW:]),
            jnp.where(last_ctx, cache_values[-WINDOW:], span_values[-WINDOW:]),
        ),
        "ctx",
        1,
    )
    reach_keys = jnp.concatenate([tail_rows[0], span_keys], axis=0)
    reach_values = jnp.concatenate([tail_rows[1], span_values], axis=0)
    gate_values = jax.nn.sigmoid(gate_logits.astype(jnp.float32)).reshape(tokens, 3, HEADS)
    offsets = jnp.arange(BLOCK, dtype=jnp.int32)
    near_offsets = jnp.arange(WINDOW + BLOCK, dtype=jnp.int32)
    slot_number = jnp.arange(reach, dtype=jnp.int32)[:, None] * owners + column_of[None, :]
    key_pos = (requested[0][:, :, None] * BLOCK + offsets).reshape(-1)
    usable = jnp.repeat((slot_number < valid_counts[0]).reshape(-1), BLOCK)
    sel_visible = usable[None, :] & (key_pos[None, :] <= row_pos[:, None])
    picked = attend(
        query_rows,
        fetched_keys[0].reshape(-1, key_width),
        fetched_values[0].reshape(-1, value_width),
        sel_visible,
        score_scale,
    )
    begin = local_start + 0
    near_keys = lax.dynamic_slice_in_dim(reach_keys, begin, WINDOW + BLOCK, 0)
    near_values = lax.dynamic_slice_in_dim(reach_values, begin, WINDOW + BLOCK, 0)
    near_pos = context_start + ctx_place * span_len - WINDOW + begin + near_offsets
    near_visible = (near_pos[None, :] <= row_pos[:, None]) & (
        near_pos[None, :] > row_pos[:, None] - WINDOW
    )
    nearby = attend(query_rows, near_keys, near_values, near_visible, score_scale)
    mixed = (
        gate_values[:, 0, :, None] * summary_out.reshape(BLOCK, HEADS, value_width)
        + gate_values[:, 1, :, None] * picked.reshape(BLOCK, HEADS, value_width)
        + gate_values[:, 2, :, None] * nearby.reshape(BLOCK, HEADS, value_width)
    )
    outputs = mixed.reshape(BLOCK, HEADS * value_width).astype(jnp.bfloat16)
    return outputs


def solution(mesh):
    return jax.shard_map(
        local,
        mesh=mesh,
        in_specs=(
            P(("parts", "ctx", "pb", "row"), None),
            P(("parts", "ctx"), None),
            P(("parts", "ctx"), None),
            P(("parts", "ctx"), None),
            P(("parts", "ctx"), None),
            P(),
            P(),
            P(("parts", "ctx", "pb", "row"), None),
            P(("parts", "ctx", "pb", "row"), None),
            P(("parts", "ctx", "pb", "row")),
        ),
        out_specs=P(("parts", "ctx", "pb", "row"), None),
        check_vma=False,
    )
```

profile of v0, /device:TPU:0, one launch (start us, length us, event | category | flops | bytes accessed | tf_op | source)
XLA Modules:
  0.0 91.8 jit_solution(5316688061465802636)
XLA Ops:
  0.0 1.3 %copy.79 = bf16[1024,192]{1,0:T(8,128)(2,1)S(1)} copy(bf16[1024,192]{0,1:T(8,128)(2,1)} %param.11) | data formatting | bytes 786432 | tf_op args[1]
  1.3 1.1 %copy.77 = bf16[512,192]{1,0:T(8,128)(2,1)S(1)} copy(bf16[512,192]{0,1:T(8,128)(2,1)} %param.13) | data formatting | bytes 393216 | tf_op args[3]
  3.0 5.1 %collective-permute-start = (bf16[16,192]{1,0:T(8,128)(2,1)}, bf16[16,192]{1,0:T(8,128)(2,1)}, u32[]{:S(2)}, u32[]{:S(2)}) collective-permute-start(bf16[16,192]{1,0:T(8,128)(2,1)} %get-tuple-element.13), channel_id=1, source_target_pairs={{0,24},{8,0},{16,8},{24,16},{1,25},{9,1},{17,9},{25,17},{2,26},{10... | collective-permute-start | bytes 18440 | tf_op jit(solution)/shard_map/ppermute | solution.py:18
  8.5 1.3 %slice_select_fusion.3 = (bf16[16,128]{1,0:T(8,128)(2,1)}, bf16[16,128]{1,0:T(8,128)(2,1)}) fusion(bf16[1024,128]{1,0:T(8,128)(2,1)} %param.12, pred[]{:T(512)S(6)} %eq.10, bf16[512,128]{1,0:T(8,128)(2,1)} %param.14), kind=kLoop, calls=%fused_computation.87 | loop fusion | flops 2048 | bytes 16385 | tf_op jit(solution)/shard_map/jit(_where)/select_n | solution.py:70
  10.8 1.3 %reduce.3 = s32[16]{0:T(128)S(1)} reduce(s32[1,16]{1,0:T(1,128)} %param.18, s32[]{:T(128)} %broadcast.494), dimensions={0}, to_apply=%param.18.reduce_sub_computation.3 | reduce | bytes 132 | tf_op args[8]
  13.7 5.3 %all-to-all-start = ((s32[1,4,4]{1,0,2:T(1,128)}), s32[1,4,4]{1,0,2:T(1,128)S(1)}, u32[]{:S(2)}, u32[]{:S(2)}) async-start(s32[1,4,4]{1,0,2:T(1,128)} %copy.85), calls=%async_computation | async-start | bytes 4096 | tf_op jit(solution)/shard_map/all_to_all | solution.py:132
  18.9 1.0 %slice_select_fusion = bf16[256,192]{0,1:T(8,128)(2,1)S(1)} fusion(bf16[512,192]{0,1:T(8,128)(2,1)} %param.13, bf16[1024,192]{0,1:T(8,128)(2,1)} %param.11, pred[]{:T(512)S(6)} %eq.11), kind=kLoop, calls=%fused_computation.60 | loop fusion | flops 49152 | bytes 294913 | tf_op jit(solution)/shard_map/jit(_where)/select_n | solution.py:155
  19.9 2.1 %collective-permute-start.4 = (bf16[256,192]{0,1:T(8,128)(2,1)S(1)}, bf16[256,192]{0,1:T(8,128)(2,1)}, u32[]{:S(2)}, u32[]{:S(2)}) collective-permute-start(bf16[256,192]{0,1:T(8,128)(2,1)S(1)} %slice_select_fusion), channel_id=1, source_target_pairs={{0,8},{8,16},{16,24},{24,0},{1,9},{9,17},{17,25},{25,1},{2,10},{10... | collective-permute-start | bytes 294920 | tf_op jit(solution)/shard_map/ppermute | solution.py:18
  30.3 0.7 copy.95
  31.1 3.6 %all-to-all-start.2 = ((bf16[1,4,4,64,128]{4,3,1,0,2:T(8,128)(2,1)}), bf16[1,4,4,64,128]{4,3,1,0,2:T(8,128)(2,1)S(1)}, u32[]{:S(2)}, u32[]{:S(2)}) async-start(bf16[1,4,4,64,128]{4,3,1,0,2:T(8,128)(2,1)} %copy.95), calls=%async_computation.2 | async-start | bytes 524288 | tf_op jit(solution)/shard_map/all_to_all | solution.py:150
  34.7 0.9 copy_select_fusion
  35.6 2.0 %collective-permute-start.5 = (bf16[256,128]{1,0:T(8,128)(2,1)S(1)}, bf16[256,128]{1,0:T(8,128)(2,1)}, u32[]{:S(2)}, u32[]{:S(2)}) collective-permute-start(bf16[256,128]{1,0:T(8,128)(2,1)S(1)} %slice_select_fusion.1), channel_id=1, source_target_pairs={{0,8},{8,16},{16,24},{24,0},{1,9},{9,17},{17,25},{25,1},{2,10},{10... | collective-permute-start | bytes 196616 | tf_op jit(solution)/shard_map/ppermute | solution.py:18
  39.6 13.2 %all_gather.7 = bf16[384,128]{1,0:T(8,128)(2,1)S(1)} all-gather(bf16[96,128]{1,0:T(8,128)(2,1)S(1)} %pad_maximum_fusion.1), channel_id=1, replica_groups=mesh['parts'=1,'ctx'=4,'pb'=4,'row'=2] {'ctx'}, dimensions={0}, use_global_device_ids=true | all-gather | bytes 122880 | tf_op jit(solution)/shard_map/all_gather | solution.py:97
  52.8 0.8 maximum_convert_fusion
  53.8 0.7 maximum_convert_fusion.1
  55.5 13.6 %all_gather.6 = bf16[384,192]{1,0:T(8,128)(2,1)S(1)} all-gather(bf16[96,192]{1,0:T(8,128)(2,1)S(1)} %pad_maximum_fusion), channel_id=1, replica_groups=mesh['parts'=1,'ctx'=4,'pb'=4,'row'=2] {'ctx'}, dimensions={0}, use_global_device_ids=true | all-gather | bytes 184320 | tf_op jit(solution)/shard_map/all_gather | solution.py:96
  70.6 3.7 %all-to-all-start.1 = ((bf16[1,4,4,64,192]{4,3,1,0,2:T(8,128)(2,1)}), bf16[1,4,4,64,192]{4,3,1,0,2:T(8,128)(2,1)S(1)}, u32[]{:S(2)}, u32[]{:S(2)}) async-start(bf16[1,4,4,64,192]{4,3,1,0,2:T(8,128)(2,1)} %copy_select_fusion), calls=%async_computation.1 | async-start | bytes 1048576 | tf_op jit(solution)/shard_map/all_to_all | solution.py:149
  74.3 1.7 %fusion.59 = (f32[1024]{0:T(1024)S(1)}, f32[1024,320]{0,1:T(8,128)S(1)}) fusion(bf16[1024,192]{1,0:T(8,128)(2,1)S(1)} %reshape.297, s32[]{:T(128)S(6)} %select_n.211, bf16[256,192]{0,1:T(8,128)(2,1)} %collective-permute-done.4, bf16[512,192]{0,1:T(8,128)(2,1)S(1)} %copy-done.2, s32[1024]{0:T(1024)S(1)} %broadcast_add_fusion, s32[1024]{0:T(1024)S(1)} %fusion.31, ...), kind=kOutput, calls=%fused_computation.137 | convolution fusion | flops 128039936 | bytes 2012420 | tf_op jit(solution)/shard_map/dot_general | solution.py:31
  76.4 1.5 %convolution_divide_fusion = f32[1024,128]{1,0:T(8,128)S(1)} fusion(f32[1024,320]{0,1:T(8,128)S(1)} %get-tuple-element.29, f32[1024]{0:T(1024)S(1)} %get-tuple-element.28, s32[1024]{0:T(1024)S(1)} %broadcast_add_fusion, s32[1024]{0:T(1024)S(1)} %fusion.31, s32[320]{0:T(512)S(1)} %iota_add_fusion.1, f32[1024]{0:T(1024)S(1)} %fusion.11, s32[]{:T(128)S(6)} %select_n.211, ...), kind=kOutput, calls=%fused_computation.21 | convolution fusion | flops 86147072 | bytes 2049284 | tf_op jit(solution)/shard_map/dot_general | solution.py:36
  78.0 6.4 %all-to-all-done.1 = bf16[1,4,4,64,192]{4,3,1,0,2:T(8,128)(2,1)S(1)} async-done(((bf16[1,4,4,64,192]{4,3,1,0,2:T(8,128)(2,1)}), bf16[1,4,4,64,192]{4,3,1,0,2:T(8,128)(2,1)S(1)}, u32[]{:S(2)}, u32[]{:S(2)}) %all-to-all-start.1) | async-done | bytes 393248 | tf_op jit(solution)/shard_map/all_to_all | solution.py:149
  84.4 1.2 %fusion = (f32[1024]{0:T(1024)S(1)}, f32[1024,1024]{1,0:T(8,128)S(1)}) fusion(s32[1024]{0:T(1024)S(1)} %fusion.31, s32[1024]{0:T(1024)S(1)} %add.265, pred[1024]{0:T(1024)(128)(4,1)S(1)} %copy-done.11, bf16[1024,192]{1,0:T(8,128)(2,1)S(1)} %bitcast.97, bf16[1024,192]{1,0:T(8,128)(2,1)S(1)} %reshape.297), kind=kOutput, calls=%fused_computation.8 | convolution fusion | flops 407895040 | bytes 4994048 | tf_op jit(solution)/shard_map/dot_general | solution.py:31
  85.6 1.9 %fusion.52 = f32[1024]{0:T(1024)S(1)} fusion(f32[1024]{0:T(1024)S(1)} %get-tuple-element.30, f32[1024,1024]{1,0:T(8,128)S(1)} %get-tuple-element.31, s32[1024]{0:T(1024)S(1)} %fusion.31, s32[1024]{0:T(1024)S(1)} %add.265, pred[1024]{0:T(1024)(128)(4,1)S(1)} %copy-done.11), kind=kLoop, calls=%fused_computation.130 | loop fusion | flops 7339008 | bytes 4211712 | tf_op jit(solution)/shard_map/reduce_sum | solution.py:37
  87.5 1.8 %fusion.6 = f32[1024,128]{1,0:T(8,128)S(1)} fusion(bf16[1024,128]{1,0:T(8,128)(2,1)S(1)} %bitcast.98, f32[1024]{0:T(1024)S(1)} %fusion.52, f32[1024,1024]{1,0:T(8,128)S(1)} %get-tuple-element.31, f32[1024]{0:T(1024)S(1)} %get-tuple-element.30, s32[1024]{0:T(1024)S(1)} %fusion.31, s32[1024]{0:T(1024)S(1)} %add.265, pred[1024]{0:T(1024)(128)(4,1)S(1)} %copy-done.11), kind=kOutput, calls=%fused_computation.20 | convolution fusion | flops 275906560 | bytes 4998144 | tf_op jit(solution)/shard_map/dot_general | solution.py:36
  90.6 1.3 %fusion.25 = bf16[64,2048]{1,0:T(8,128)(2,1)} fusion(f32[64,2048]{1,0:T(8,128)S(1)} %reshape.305, f32[8,8,16,128]{3,2,1,0:T(8,128)S(1)} %bitcast.92, f32[64,2048]{1,0:T(8,128)S(1)} %reshape.304, f32[8,8,16,128]{3,2,1,0:T(8,128)S(1)} %bitcast.91, f32[64,2048]{1,0:T(8,128)S(1)} %reshape.298, f32[8,8,16,128]{3,2,1,0:T(8,128)S(1)} %bitcast.90), kind=kLoop, calls=%fused_computation.40 | loop fusion | flops 786432 | bytes 3407872 | tf_op jit(solution)/shard_map/convert_element_type | solution.py:190
  (115 shorter events, 17.3 us)
Async XLA Ops:
  0.0 22.7 %copy-start.1 = (bf16[1024,128]{1,0:T(8,128)(2,1)S(1)}, bf16[1024,128]{1,0:T(8,128)(2,1)}, u32[]{:S(2)}) copy-start(bf16[1024,128]{1,0:T(8,128)(2,1)} %param.12) | copy-start | bytes 786436
  0.0 22.7 %copy-start = (bf16[512,128]{1,0:T(8,128)(2,1)S(1)}, bf16[512,128]{1,0:T(8,128)(2,1)}, u32[]{:S(2)}) copy-start(bf16[512,128]{1,0:T(8,128)(2,1)} %param.14) | copy-start | bytes 393220
  0.0 22.7 %copy-start.7 = (f32[32,192]{1,0:T(8,128)S(1)}, f32[32,192]{1,0:T(8,128)}, u32[]{:S(2)}) copy-start(f32[32,192]{1,0:T(8,128)} %param.15) | copy-start | bytes 73732
  0.0 22.7 %copy-start.3 = (bf16[64,3072]{1,0:T(8,128)(2,1)S(1)}, bf16[64,3072]{1,0:T(8,128)(2,1)}, u32[]{:S(2)}) copy-start(bf16[64,3072]{1,0:T(8,128)(2,1)} %param.10) | copy-start | bytes 1179652
  0.0 23.4 %copy-start.8 = (f32[32,128]{1,0:T(8,128)S(1)}, f32[32,128]{1,0:T(8,128)}, u32[]{:S(2)}) copy-start(f32[32,128]{1,0:T(8,128)} %param.16) | copy-start | bytes 49156
  0.0 25.2 %copy-start.9 = (bf16[64,48]{0,1:T(8,128)(2,1)S(1)}, bf16[64,48]{0,1:T(8,128)(2,1)}, u32[]{:S(2)}) copy-start(bf16[64,48]{0,1:T(8,128)(2,1)} %param.17) | copy-start | bytes 18436
  3.0 49.8 %collective-permute-start = (bf16[16,192]{1,0:T(8,128)(2,1)}, bf16[16,192]{1,0:T(8,128)(2,1)}, u32[]{:S(2)}, u32[]{:S(2)}) collective-permute-start(bf16[16,192]{1,0:T(8,128)(2,1)} %get-tuple-element.13), channel_id=1, source_target_pairs={{0,24},{8,0},{16,8},{24,16},{1,25},{9,1},{17,9},{25,17},{2,26},{10... | collective-permute-start | bytes 18440 | tf_op jit(solution)/shard_map/ppermute | solution.py:18
  8.0 45.7 %collective-permute-start.1 = (bf16[16,192]{1,0:T(8,128)(2,1)}, bf16[16,192]{1,0:T(8,128)(2,1)}, u32[]{:S(2)}, u32[]{:S(2)}) collective-permute-start(bf16[16,192]{1,0:T(8,128)(2,1)} %get-tuple-element.14), channel_id=1, source_target_pairs={{0,24},{8,0},{16,8},{24,16},{1,25},{9,1},{17,9},{25,17},{2,26},{10... | collective-permute-start | bytes 18440 | tf_op jit(solution)/shard_map/ppermute | solution.py:18
  9.8 25.8 %collective-permute-start.2 = (bf16[16,128]{1,0:T(8,128)(2,1)}, bf16[16,128]{1,0:T(8,128)(2,1)}, u32[]{:S(2)}, u32[]{:S(2)}) collective-permute-start(bf16[16,128]{1,0:T(8,128)(2,1)} %get-tuple-element.15), channel_id=1, source_target_pairs={{0,24},{8,0},{16,8},{24,16},{1,25},{9,1},{17,9},{25,17},{2,26},{10... | collective-permute-start | bytes 12296 | tf_op jit(solution)/shard_map/ppermute | solution.py:18
  10.2 28.2 %collective-permute-start.3 = (bf16[16,128]{1,0:T(8,128)(2,1)}, bf16[16,128]{1,0:T(8,128)(2,1)}, u32[]{:S(2)}, u32[]{:S(2)}) collective-permute-start(bf16[16,128]{1,0:T(8,128)(2,1)} %get-tuple-element.16), channel_id=1, source_target_pairs={{0,24},{8,0},{16,8},{24,16},{1,25},{9,1},{17,9},{25,17},{2,26},{10... | collective-permute-start | bytes 12296 | tf_op jit(solution)/shard_map/ppermute | solution.py:18
  13.7 13.6 %all-to-all-start = ((s32[1,4,4]{1,0,2:T(1,128)}), s32[1,4,4]{1,0,2:T(1,128)S(1)}, u32[]{:S(2)}, u32[]{:S(2)}) async-start(s32[1,4,4]{1,0,2:T(1,128)} %copy.85), calls=%async_computation | async-start | bytes 4096 | tf_op jit(solution)/shard_map/all_to_all | solution.py:132
  19.9 54.4 %collective-permute-start.4 = (bf16[256,192]{0,1:T(8,128)(2,1)S(1)}, bf16[256,192]{0,1:T(8,128)(2,1)}, u32[]{:S(2)}, u32[]{:S(2)}) collective-permute-start(bf16[256,192]{0,1:T(8,128)(2,1)S(1)} %slice_select_fusion), channel_id=1, source_target_pairs={{0,8},{8,16},{16,24},{24,0},{1,9},{9,17},{17,25},{25,1},{2,10},{10... | collective-permute-start | bytes 294920 | tf_op jit(solution)/shard_map/ppermute | solution.py:18
  31.1 39.6 %all-to-all-start.2 = ((bf16[1,4,4,64,128]{4,3,1,0,2:T(8,128)(2,1)}), bf16[1,4,4,64,128]{4,3,1,0,2:T(8,128)(2,1)S(1)}, u32[]{:S(2)}, u32[]{:S(2)}) async-start(bf16[1,4,4,64,128]{4,3,1,0,2:T(8,128)(2,1)} %copy.95), calls=%async_computation.2 | async-start | bytes 524288 | tf_op jit(solution)/shard_map/all_to_all | solution.py:150
  35.6 40.8 %collective-permute-start.5 = (bf16[256,128]{1,0:T(8,128)(2,1)S(1)}, bf16[256,128]{1,0:T(8,128)(2,1)}, u32[]{:S(2)}, u32[]{:S(2)}) collective-permute-start(bf16[256,128]{1,0:T(8,128)(2,1)S(1)} %slice_select_fusion.1), channel_id=1, source_target_pairs={{0,8},{8,16},{16,24},{24,0},{1,9},{9,17},{17,25},{25,1},{2,10},{10... | collective-permute-start | bytes 196616 | tf_op jit(solution)/shard_map/ppermute | solution.py:18
  54.6 14.4 %copy-start.10 = (s32[384]{0:T(512)S(1)}, s32[384]{0:T(512)}, u32[]{:S(2)}) copy-start(s32[384]{0:T(512)} %multiply_add_fusion) | copy-start | bytes 4612
  70.5 3.8 %copy-start.2 = (bf16[512,192]{0,1:T(8,128)(2,1)S(1)}, bf16[512,192]{0,1:T(8,128)(2,1)}, u32[]{:S(2)}) copy-start(bf16[512,192]{0,1:T(8,128)(2,1)} %param.13) | copy-start | bytes 589828
  70.6 13.7 %all-to-all-start.1 = ((bf16[1,4,4,64,192]{4,3,1,0,2:T(8,128)(2,1)}), bf16[1,4,4,64,192]{4,3,1,0,2:T(8,128)(2,1)S(1)}, u32[]{:S(2)}, u32[]{:S(2)}) async-start(bf16[1,4,4,64,192]{4,3,1,0,2:T(8,128)(2,1)} %copy_select_fusion), calls=%async_computation.1 | async-start | bytes 1048576 | tf_op jit(solution)/shard_map/all_to_all | solution.py:149
  77.9 6.5 %copy-start.11 = (pred[1024]{0:T(1024)(128)(4,1)S(1)}, pred[1024]{0:T(1024)(128)(4,1)}, u32[]{:S(2)}) copy-start(pred[1024]{0:T(1024)(128)(4,1)} %and.99) | copy-start | bytes 3076
  87.5 2.0 %copy-start.4 = (f32[64,16]{1,0:T(8,128)S(1)}, f32[64,16]{1,0:T(8,128)}, u32[]{:S(2)}) copy-start(f32[64,16]{1,0:T(8,128)} %copy.76) | copy-start | bytes 12292
  89.4 0.8 copy-start.5
  89.4 0.9 %copy-start.6 = (f32[64,16]{1,0:T(8,128)S(1)}, f32[64,16]{1,0:T(8,128)}, u32[]{:S(2)}) copy-start(f32[64,16]{1,0:T(8,128)} %copy.97) | copy-start | bytes 12292
where the time goes:
time: 92.6 us; the launch traced here: 91.8 us
  blocking collectives  26.8 us (29%)
  starting transfers between devices  22.7 us (25%)
  other arithmetic  14.1 us (15%)
  local copies, waits for them, and re-layouts  13.3 us (14%)
  matrix products  7.31 us (8%)
  waiting for transfers between devices  6.38 us (7%)
  between operations  1.25 us (1%)
    all_gather x1, blocking collectives, local(): part_keys = lax.all_gather(summary_keys, 'ctx', axis=0, tiled=True)  13.6 us
    all_gather x1, blocking collectives, local(): part_values = lax.all_gather(summary_values, 'ctx', axis=0, tiled=True)  13.2 us
    ppermute x6, starting transfers between devices, from_behind(): return lax.ppermute(value, axis, pairs)  10.1 us
    all_to_all x1, waiting for transfers between devices, local(): lax.all_to_all(served_keys, 'ctx', split_axis=2, concat_axis=2, tiled=True)  6.36 us
    all_to_all x1, starting transfers between devices, local(): lax.all_to_all(requested, 'ctx', split_axis=2, concat_axis=2, tiled=True)  5.27 us
    all_to_all x1, starting transfers between devices, local(): lax.all_to_all(served_keys, 'ctx', split_axis=2, concat_axis=2, tiled=True)  3.66 us
    all_to_all x1, starting transfers between devices, local(): lax.all_to_all(served_values, 'ctx', split_axis=2, concat_axis=2, tiled=T...  3.63 us
    unnamed x27, local copies, waits for them, and re-layouts  3.33 us
  transfers between devices with their start and end apart: 9, of which 1 were waited for; matrix products, arithmetic and copies ran while one was open for 27% of the time, Pallas kernels for 0%

commit v1 on v0

--- a/solution.py
+++ b/solution.py
@@ -94,7 +94,15 @@
     running_sum = jnp.zeros((row_count,), jnp.float32)
     running_out = jnp.zeros((row_count, value_width), jnp.float32)
     part_keys = lax.all_gather(summary_keys, "ctx", axis=0, tiled=True)
-    part_values = lax.all_gather(summary_values, "ctx", axis=0, tiled=True)
+    ways, here = (lax.axis_size("ctx"), lax.axis_index("ctx"))
+    grown, reach_2 = (summary_values, 1)
+    while reach_2 < ways:
+        theirs = lax.ppermute(grown, "ctx", [(d, d ^ reach_2) for d in range(ways)])
+        mine_first = jnp.concatenate([grown, theirs], axis=0)
+        theirs_first = jnp.concatenate([theirs, grown], axis=0)
+        grown = jnp.where(here & reach_2 == 0, mine_first, theirs_first)
+        reach_2 = 2 * reach_2
+    part_values = grown
     length = part_keys.shape[0]
     for lower_row in range(0, length, 512):
         upper_row = min(lower_row + 512, length)

time: 92.6 us -> 87.1 us (0.941)
  blocking collectives: 26.8 us -> 13.6 us
  waiting for transfers between devices: 6.38 us -> 11.2 us
  starting transfers between devices: 22.7 us -> 24.9 us
    all_gather x1 -> x0, blocking collectives: 13.2 us -> none  [local(): part_values = lax.all_gather(summary_values, 'ctx', axis=0, tiled=True)]
    ppermute x0 -> x2, waiting for transfers between devices: none -> 4.88 us  [local(): theirs = lax.ppermute(grown, 'ctx', [(d, d ^ reach_2) for d in range(ways)])]
    ppermute x0 -> x2, starting transfers between devices: none -> 2.22 us  [local(): theirs = lax.ppermute(grown, 'ctx', [(d, d ^ reach_2) for d in range(ways)])]
    unnamed x27 -> x29, local copies, waits for them, and re-layouts: 3.33 us -> 3.33 us
  transfers between devices with their start and end apart: 9 -> 11, of which waited for: 1 -> 2; matrix products, arithmetic and copies ran while one was open for 27% -> 29% of each run, Pallas kernels for 0% -> 0%
where the time goes in v1:
time: 87.1 us; the launch traced here: 86.4 us
  starting transfers between devices  24.9 us (29%)
  other arithmetic  14.7 us (17%)
  blocking collectives  13.6 us (16%)
  local copies, waits for them, and re-layouts  13.4 us (15%)
  waiting for transfers between devices  11.2 us (13%)
  matrix products  7.33 us (8%)
  between operations  1.28 us (1%)
    all_gather x1, blocking collectives, local(): part_keys = lax.all_gather(summary_keys, 'ctx', axis=0, tiled=True)  13.6 us
    ppermute x6, starting transfers between devices, from_behind(): return lax.ppermute(value, axis, pairs)  10.1 us
    all_to_all x1, waiting for transfers between devices, local(): lax.all_to_all(served_keys, 'ctx', split_axis=2, concat_axis=2, tiled=True)  6.34 us
    all_to_all x1, starting transfers between devices, local(): lax.all_to_all(requested, 'ctx', split_axis=2, concat_axis=2, tiled=True)  5.27 us
    ppermute x2, waiting for transfers between devices, local(): theirs = lax.ppermute(grown, 'ctx', [(d, d ^ reach_2) for d in range(ways)])  4.88 us
    all_to_all x1, starting transfers between devices, local(): lax.all_to_all(served_keys, 'ctx', split_axis=2, concat_axis=2, tiled=True)  3.66 us
    all_to_all x1, starting transfers between devices, local(): lax.all_to_all(served_values, 'ctx', split_axis=2, concat_axis=2, tiled=T...  3.63 us
    unnamed x29, local copies, waits for them, and re-layouts  3.33 us
  transfers between devices with their start and end apart: 11, of which 2 were waited for; matrix products, arithmetic and copies ran while one was open for 29% of the time, Pallas kernels for 0%

profile of v1, /device:TPU:0, one launch (start us, length us, event | category | flops | bytes accessed | tf_op | source)
XLA Modules:
  0.0 86.4 jit_solution(10716105018812927314)
XLA Ops:
  0.0 1.3 %copy.79 = bf16[1024,192]{1,0:T(8,128)(2,1)S(1)} copy(bf16[1024,192]{0,1:T(8,128)(2,1)} %param.11) | data formatting | bytes 786432 | tf_op args[1]
  1.3 1.1 %copy.77 = bf16[512,192]{1,0:T(8,128)(2,1)S(1)} copy(bf16[512,192]{0,1:T(8,128)(2,1)} %param.13) | data formatting | bytes 393216 | tf_op args[3]
  3.0 5.1 %collective-permute-start = (bf16[16,192]{1,0:T(8,128)(2,1)}, bf16[16,192]{1,0:T(8,128)(2,1)}, u32[]{:S(2)}, u32[]{:S(2)}) collective-permute-start(bf16[16,192]{1,0:T(8,128)(2,1)} %get-tuple-element.13), channel_id=1, source_target_pairs={{0,24},{8,0},{16,8},{24,16},{1,25},{9,1},{17,9},{25,17},{2,26},{10... | collective-permute-start | bytes 18440 | tf_op jit(solution)/shard_map/ppermute | solution.py:18
  8.5 1.3 %slice_select_fusion.3 = (bf16[16,128]{1,0:T(8,128)(2,1)}, bf16[16,128]{1,0:T(8,128)(2,1)}) fusion(bf16[1024,128]{1,0:T(8,128)(2,1)} %param.12, pred[]{:T(512)S(6)} %eq.16, bf16[512,128]{1,0:T(8,128)(2,1)} %param.14), kind=kLoop, calls=%fused_computation.95 | loop fusion | flops 2048 | bytes 16385 | tf_op jit(solution)/shard_map/jit(_where)/select_n | solution.py:70
  10.8 1.3 %reduce.3 = s32[16]{0:T(128)S(1)} reduce(s32[1,16]{1,0:T(1,128)} %param.18, s32[]{:T(128)} %broadcast.494), dimensions={0}, to_apply=%param.18.reduce_sub_computation.3 | reduce | bytes 132 | tf_op args[8]
  13.7 5.3 %all-to-all-start = ((s32[1,4,4]{1,0,2:T(1,128)}), s32[1,4,4]{1,0,2:T(1,128)S(1)}, u32[]{:S(2)}, u32[]{:S(2)}) async-start(s32[1,4,4]{1,0,2:T(1,128)} %copy.85), calls=%async_computation | async-start | bytes 4096 | tf_op jit(solution)/shard_map/all_to_all | solution.py:140
  18.9 1.0 %slice_select_fusion = bf16[256,192]{0,1:T(8,128)(2,1)S(1)} fusion(bf16[512,192]{0,1:T(8,128)(2,1)} %param.13, bf16[1024,192]{0,1:T(8,128)(2,1)} %param.11, pred[]{:T(512)S(6)} %eq.19), kind=kLoop, calls=%fused_computation.66 | loop fusion | flops 49152 | bytes 294913 | tf_op jit(solution)/shard_map/jit(_where)/select_n | solution.py:163
  19.9 2.1 %collective-permute-start.6 = (bf16[256,192]{0,1:T(8,128)(2,1)S(1)}, bf16[256,192]{0,1:T(8,128)(2,1)}, u32[]{:S(2)}, u32[]{:S(2)}) collective-permute-start(bf16[256,192]{0,1:T(8,128)(2,1)S(1)} %slice_select_fusion), channel_id=1, source_target_pairs={{0,8},{8,16},{16,24},{24,0},{1,9},{9,17},{17,25},{25,1},{2,10},{10... | collective-permute-start | bytes 294920 | tf_op jit(solution)/shard_map/ppermute | solution.py:18
  31.7 3.6 %all-to-all-start.2 = ((bf16[1,4,4,64,128]{4,3,1,0,2:T(8,128)(2,1)}), bf16[1,4,4,64,128]{4,3,1,0,2:T(8,128)(2,1)S(1)}, u32[]{:S(2)}, u32[]{:S(2)}) async-start(bf16[1,4,4,64,128]{4,3,1,0,2:T(8,128)(2,1)} %copy.95), calls=%async_computation.2 | async-start | bytes 524288 | tf_op jit(solution)/shard_map/all_to_all | solution.py:158
  35.4 0.9 %copy_select_fusion = bf16[1,4,4,64,192]{4,3,1,0,2:T(8,128)(2,1)} fusion(bf16[1,4,4,64,192]{4,3,2,1,0:T(8,128)(2,1)S(1)} %bitcast.88, bf16[1,4,4,64,192]{4,3,2,1,0:T(8,128)(2,1)S(1)} %bitcast.87, pred[4,4]{0,1:T(4,128)(4,1)S(1)} %copy.87), kind=kLoop, calls=%fused_computation.44 | loop fusion | flops 196608 | bytes 1179664 | tf_op jit(solution)/shard_map/jit(_where)/select_n | solution.py:146
  36.3 2.0 %collective-permute-start.7 = (bf16[256,128]{1,0:T(8,128)(2,1)S(1)}, bf16[256,128]{1,0:T(8,128)(2,1)}, u32[]{:S(2)}, u32[]{:S(2)}) collective-permute-start(bf16[256,128]{1,0:T(8,128)(2,1)S(1)} %slice_select_fusion.1), channel_id=1, source_target_pairs={{0,8},{8,16},{16,24},{24,0},{1,9},{9,17},{17,25},{25,1},{2,10},{10... | collective-permute-start | bytes 196616 | tf_op jit(solution)/shard_map/ppermute | solution.py:18
  40.2 1.5 %collective-permute-start.4 = (bf16[96,128]{1,0:T(8,128)(2,1)S(1)}, bf16[96,128]{1,0:T(8,128)(2,1)S(1)}, u32[]{:S(2)}, u32[]{:S(2)}) collective-permute-start(bf16[96,128]{1,0:T(8,128)(2,1)S(1)} %pad_maximum_fusion.1), channel_id=1, source_target_pairs={{0,8},{8,0},{16,24},{24,16},{1,9},{9,1},{17,25},{25,17},{2,10},{10... | collective-permute-start | bytes 73736 | tf_op jit(solution)/shard_map/ppermute | solution.py:100
  41.8 0.8 maximum_convert_fusion
  42.7 0.7 maximum_convert_fusion.1
  44.4 13.6 %all_gather.3 = bf16[384,192]{1,0:T(8,128)(2,1)S(1)} all-gather(bf16[96,192]{1,0:T(8,128)(2,1)S(1)} %pad_maximum_fusion), channel_id=1, replica_groups=mesh['parts'=1,'ctx'=4,'pb'=4,'row'=2] {'ctx'}, dimensions={0}, use_global_device_ids=true | all-gather | bytes 184320 | tf_op jit(solution)/shard_map/all_gather | solution.py:96
  59.5 4.9 %collective-permute-done.5 = bf16[192,128]{1,0:T(8,128)(2,1)S(1)} collective-permute-done((bf16[192,128]{1,0:T(8,128)(2,1)S(1)}, bf16[192,128]{1,0:T(8,128)(2,1)S(1)}, u32[]{:S(2)}, u32[]{:S(2)}) %collective-permute-start.5) | collective-permute-done | bytes 49184 | tf_op jit(solution)/shard_map/ppermute | solution.py:100
  65.2 3.7 %all-to-all-start.1 = ((bf16[1,4,4,64,192]{4,3,1,0,2:T(8,128)(2,1)}), bf16[1,4,4,64,192]{4,3,1,0,2:T(8,128)(2,1)S(1)}, u32[]{:S(2)}, u32[]{:S(2)}) async-start(bf16[1,4,4,64,192]{4,3,1,0,2:T(8,128)(2,1)} %copy_select_fusion), calls=%async_computation.1 | async-start | bytes 1048576 | tf_op jit(solution)/shard_map/all_to_all | solution.py:157
  68.9 1.7 %fusion.66 = (f32[1024]{0:T(1024)S(1)}, f32[1024,320]{0,1:T(8,128)S(1)}) fusion(bf16[1024,192]{1,0:T(8,128)(2,1)S(1)} %reshape.297, s32[]{:T(128)S(6)} %select_n.231, bf16[256,192]{0,1:T(8,128)(2,1)} %collective-permute-done.6, bf16[512,192]{0,1:T(8,128)(2,1)S(1)} %copy-done.2, s32[1024]{0:T(1024)S(1)} %broadcast_add_fusion, s32[1024]{0:T(1024)S(1)} %fusion.37, ...), kind=kOutput, calls=%fused_computation.146 | convolution fusion | flops 128039936 | bytes 2012420 | tf_op jit(solution)/shard_map/dot_general | solution.py:31
  71.0 1.5 %convolution_divide_fusion = f32[1024,128]{1,0:T(8,128)S(1)} fusion(f32[1024,320]{0,1:T(8,128)S(1)} %get-tuple-element.29, f32[1024]{0:T(1024)S(1)} %get-tuple-element.28, s32[1024]{0:T(1024)S(1)} %broadcast_add_fusion, s32[1024]{0:T(1024)S(1)} %fusion.37, s32[320]{0:T(512)S(1)} %copy-done.10, f32[1024]{0:T(1024)S(1)} %fusion.11, s32[]{:T(128)S(6)} %select_n.231, ...), kind=kOutput, calls=%fused_computation.21 | convolution fusion | flops 86147072 | bytes 2049284 | tf_op jit(solution)/shard_map/dot_general | solution.py:36
  72.6 6.3 %all-to-all-done.1 = bf16[1,4,4,64,192]{4,3,1,0,2:T(8,128)(2,1)S(1)} async-done(((bf16[1,4,4,64,192]{4,3,1,0,2:T(8,128)(2,1)}), bf16[1,4,4,64,192]{4,3,1,0,2:T(8,128)(2,1)S(1)}, u32[]{:S(2)}, u32[]{:S(2)}) %all-to-all-start.1) | async-done | bytes 393248 | tf_op jit(solution)/shard_map/all_to_all | solution.py:157
  79.0 1.2 %fusion = (f32[1024]{0:T(1024)S(1)}, f32[1024,1024]{1,0:T(8,128)S(1)}) fusion(s32[1024]{0:T(1024)S(1)} %fusion.37, s32[1024]{0:T(1024)S(1)} %add.265, pred[1024]{0:T(1024)(128)(4,1)S(1)} %copy-done.12, bf16[1024,192]{1,0:T(8,128)(2,1)S(1)} %bitcast.96, bf16[1024,192]{1,0:T(8,128)(2,1)S(1)} %reshape.297), kind=kOutput, calls=%fused_computation.8 | convolution fusion | flops 407895040 | bytes 4994048 | tf_op jit(solution)/shard_map/dot_general | solution.py:31
  80.2 1.9 %fusion.59 = f32[1024]{0:T(1024)S(1)} fusion(f32[1024]{0:T(1024)S(1)} %get-tuple-element.30, f32[1024,1024]{1,0:T(8,128)S(1)} %get-tuple-element.31, s32[1024]{0:T(1024)S(1)} %fusion.37, s32[1024]{0:T(1024)S(1)} %add.265, pred[1024]{0:T(1024)(128)(4,1)S(1)} %copy-done.12), kind=kLoop, calls=%fused_computation.139 | loop fusion | flops 7339008 | bytes 4211712 | tf_op jit(solution)/shard_map/reduce_sum | solution.py:37
  82.1 1.8 %fusion.6 = f32[1024,128]{1,0:T(8,128)S(1)} fusion(bf16[1024,128]{1,0:T(8,128)(2,1)S(1)} %bitcast.97, f32[1024]{0:T(1024)S(1)} %fusion.59, f32[1024,1024]{1,0:T(8,128)S(1)} %get-tuple-element.31, f32[1024]{0:T(1024)S(1)} %get-tuple-element.30, s32[1024]{0:T(1024)S(1)} %fusion.37, s32[1024]{0:T(1024)S(1)} %add.265, pred[1024]{0:T(1024)(128)(4,1)S(1)} %copy-done.12), kind=kOutput, calls=%fused_computation.20 | convolution fusion | flops 275906560 | bytes 4998144 | tf_op jit(solution)/shard_map/dot_general | solution.py:36
  85.1 1.3 %fusion.25 = bf16[64,2048]{1,0:T(8,128)(2,1)} fusion(f32[64,2048]{1,0:T(8,128)S(1)} %reshape.305, f32[8,8,16,128]{3,2,1,0:T(8,128)S(1)} %bitcast.91, f32[64,2048]{1,0:T(8,128)S(1)} %reshape.304, f32[8,8,16,128]{3,2,1,0:T(8,128)S(1)} %bitcast.90, f32[64,2048]{1,0:T(8,128)S(1)} %reshape.298, f32[8,8,16,128]{3,2,1,0:T(8,128)S(1)} %bitcast.89), kind=kLoop, calls=%fused_computation.40 | loop fusion | flops 786432 | bytes 3407872 | tf_op jit(solution)/shard_map/convert_element_type | solution.py:198
  (121 shorter events, 19.4 us)
Async XLA Ops:
  0.0 22.7 %copy-start.1 = (bf16[1024,128]{1,0:T(8,128)(2,1)S(1)}, bf16[1024,128]{1,0:T(8,128)(2,1)}, u32[]{:S(2)}) copy-start(bf16[1024,128]{1,0:T(8,128)(2,1)} %param.12) | copy-start | bytes 786436
  0.0 22.7 %copy-start = (bf16[512,128]{1,0:T(8,128)(2,1)S(1)}, bf16[512,128]{1,0:T(8,128)(2,1)}, u32[]{:S(2)}) copy-start(bf16[512,128]{1,0:T(8,128)(2,1)} %param.14) | copy-start | bytes 393220
  0.0 22.7 %copy-start.7 = (f32[32,192]{1,0:T(8,128)S(1)}, f32[32,192]{1,0:T(8,128)}, u32[]{:S(2)}) copy-start(f32[32,192]{1,0:T(8,128)} %param.15) | copy-start | bytes 73732
  0.0 22.8 %copy-start.3 = (bf16[64,3072]{1,0:T(8,128)(2,1)S(1)}, bf16[64,3072]{1,0:T(8,128)(2,1)}, u32[]{:S(2)}) copy-start(bf16[64,3072]{1,0:T(8,128)(2,1)} %param.10) | copy-start | bytes 1179652
  0.0 23.4 %copy-start.8 = (f32[32,128]{1,0:T(8,128)S(1)}, f32[32,128]{1,0:T(8,128)}, u32[]{:S(2)}) copy-start(f32[32,128]{1,0:T(8,128)} %param.16) | copy-start | bytes 49156
  0.0 25.8 %copy-start.9 = (bf16[64,48]{0,1:T(8,128)(2,1)S(1)}, bf16[64,48]{0,1:T(8,128)(2,1)}, u32[]{:S(2)}) copy-start(bf16[64,48]{0,1:T(8,128)(2,1)} %param.17) | copy-start | bytes 18436
  3.0 38.8 %collective-permute-start = (bf16[16,192]{1,0:T(8,128)(2,1)}, bf16[16,192]{1,0:T(8,128)(2,1)}, u32[]{:S(2)}, u32[]{:S(2)}) collective-permute-start(bf16[16,192]{1,0:T(8,128)(2,1)} %get-tuple-element.13), channel_id=1, source_target_pairs={{0,24},{8,0},{16,8},{24,16},{1,25},{9,1},{17,9},{25,17},{2,26},{10... | collective-permute-start | bytes 18440 | tf_op jit(solution)/shard_map/ppermute | solution.py:18
  8.0 34.7 %collective-permute-start.1 = (bf16[16,192]{1,0:T(8,128)(2,1)}, bf16[16,192]{1,0:T(8,128)(2,1)}, u32[]{:S(2)}, u32[]{:S(2)}) collective-permute-start(bf16[16,192]{1,0:T(8,128)(2,1)} %get-tuple-element.14), channel_id=1, source_target_pairs={{0,24},{8,0},{16,8},{24,16},{1,25},{9,1},{17,9},{25,17},{2,26},{10... | collective-permute-start | bytes 18440 | tf_op jit(solution)/shard_map/ppermute | solution.py:18
  9.8 26.5 %collective-permute-start.2 = (bf16[16,128]{1,0:T(8,128)(2,1)}, bf16[16,128]{1,0:T(8,128)(2,1)}, u32[]{:S(2)}, u32[]{:S(2)}) collective-permute-start(bf16[16,128]{1,0:T(8,128)(2,1)} %get-tuple-element.15), channel_id=1, source_target_pairs={{0,24},{8,0},{16,8},{24,16},{1,25},{9,1},{17,9},{25,17},{2,26},{10... | collective-permute-start | bytes 12296 | tf_op jit(solution)/shard_map/ppermute | solution.py:18
  10.2 28.8 %collective-permute-start.3 = (bf16[16,128]{1,0:T(8,128)(2,1)}, bf16[16,128]{1,0:T(8,128)(2,1)}, u32[]{:S(2)}, u32[]{:S(2)}) collective-permute-start(bf16[16,128]{1,0:T(8,128)(2,1)} %get-tuple-element.16), channel_id=1, source_target_pairs={{0,24},{8,0},{16,8},{24,16},{1,25},{9,1},{17,9},{25,17},{2,26},{10... | collective-permute-start | bytes 12296 | tf_op jit(solution)/shard_map/ppermute | solution.py:18
  13.7 14.2 %all-to-all-start = ((s32[1,4,4]{1,0,2:T(1,128)}), s32[1,4,4]{1,0,2:T(1,128)S(1)}, u32[]{:S(2)}, u32[]{:S(2)}) async-start(s32[1,4,4]{1,0,2:T(1,128)} %copy.85), calls=%async_computation | async-start | bytes 4096 | tf_op jit(solution)/shard_map/all_to_all | solution.py:140
  19.9 48.9 %collective-permute-start.6 = (bf16[256,192]{0,1:T(8,128)(2,1)S(1)}, bf16[256,192]{0,1:T(8,128)(2,1)}, u32[]{:S(2)}, u32[]{:S(2)}) collective-permute-start(bf16[256,192]{0,1:T(8,128)(2,1)S(1)} %slice_select_fusion), channel_id=1, source_target_pairs={{0,8},{8,16},{16,24},{24,0},{1,9},{9,17},{17,25},{25,1},{2,10},{10... | collective-permute-start | bytes 294920 | tf_op jit(solution)/shard_map/ppermute | solution.py:18
  31.7 33.4 %all-to-all-start.2 = ((bf16[1,4,4,64,128]{4,3,1,0,2:T(8,128)(2,1)}), bf16[1,4,4,64,128]{4,3,1,0,2:T(8,128)(2,1)S(1)}, u32[]{:S(2)}, u32[]{:S(2)}) async-start(bf16[1,4,4,64,128]{4,3,1,0,2:T(8,128)(2,1)} %copy.95), calls=%async_computation.2 | async-start | bytes 524288 | tf_op jit(solution)/shard_map/all_to_all | solution.py:158
  36.3 34.7 %collective-permute-start.7 = (bf16[256,128]{1,0:T(8,128)(2,1)S(1)}, bf16[256,128]{1,0:T(8,128)(2,1)}, u32[]{:S(2)}, u32[]{:S(2)}) collective-permute-start(bf16[256,128]{1,0:T(8,128)(2,1)S(1)} %slice_select_fusion.1), channel_id=1, source_target_pairs={{0,8},{8,16},{16,24},{24,0},{1,9},{9,17},{17,25},{25,1},{2,10},{10... | collective-permute-start | bytes 196616 | tf_op jit(solution)/shard_map/ppermute | solution.py:18
  40.2 18.5 %collective-permute-start.4 = (bf16[96,128]{1,0:T(8,128)(2,1)S(1)}, bf16[96,128]{1,0:T(8,128)(2,1)S(1)}, u32[]{:S(2)}, u32[]{:S(2)}) collective-permute-start(bf16[96,128]{1,0:T(8,128)(2,1)S(1)} %pad_maximum_fusion.1), channel_id=1, source_target_pairs={{0,8},{8,0},{16,24},{24,16},{1,9},{9,1},{17,25},{25,17},{2,10},{10... | collective-permute-start | bytes 73736 | tf_op jit(solution)/shard_map/ppermute | solution.py:100
  43.5 14.4 %copy-start.11 = (s32[384]{0:T(512)S(1)}, s32[384]{0:T(512)}, u32[]{:S(2)}) copy-start(s32[384]{0:T(512)} %multiply_add_fusion) | copy-start | bytes 4612
  58.8 5.6 %collective-permute-start.5 = (bf16[192,128]{1,0:T(8,128)(2,1)S(1)}, bf16[192,128]{1,0:T(8,128)(2,1)S(1)}, u32[]{:S(2)}, u32[]{:S(2)}) collective-permute-start(bf16[192,128]{1,0:T(8,128)(2,1)S(1)} %maximum_select_fusion.2), channel_id=1, source_target_pairs={{0,16},{8,24},{16,0},{24,8},{1,17},{9,25},{17,1},{25,9},{2,18},{10... | collective-permute-start | bytes 147464 | tf_op jit(solution)/shard_map/ppermute | solution.py:100
  65.1 3.8 %copy-start.2 = (bf16[512,192]{0,1:T(8,128)(2,1)S(1)}, bf16[512,192]{0,1:T(8,128)(2,1)}, u32[]{:S(2)}) copy-start(bf16[512,192]{0,1:T(8,128)(2,1)} %param.13) | copy-start | bytes 589828
  65.1 3.8 %copy-start.10 = (s32[320]{0:T(512)S(1)}, s32[320]{0:T(512)}, u32[]{:S(2)}) copy-start(s32[320]{0:T(512)} %iota_add_fusion.1) | copy-start | bytes 3844
  65.2 13.7 %all-to-all-start.1 = ((bf16[1,4,4,64,192]{4,3,1,0,2:T(8,128)(2,1)}), bf16[1,4,4,64,192]{4,3,1,0,2:T(8,128)(2,1)S(1)}, u32[]{:S(2)}, u32[]{:S(2)}) async-start(bf16[1,4,4,64,192]{4,3,1,0,2:T(8,128)(2,1)} %copy_select_fusion), calls=%async_computation.1 | async-start | bytes 1048576 | tf_op jit(solution)/shard_map/all_to_all | solution.py:157
  72.4 6.5 %copy-start.12 = (pred[1024]{0:T(1024)(128)(4,1)S(1)}, pred[1024]{0:T(1024)(128)(4,1)}, u32[]{:S(2)}) copy-start(pred[1024]{0:T(1024)(128)(4,1)} %and.107) | copy-start | bytes 3076
  82.1 2.0 %copy-start.4 = (f32[64,16]{1,0:T(8,128)S(1)}, f32[64,16]{1,0:T(8,128)}, u32[]{:S(2)}) copy-start(f32[64,16]{1,0:T(8,128)} %copy.76) | copy-start | bytes 12292
  83.9 0.8 copy-start.5
  84.0 0.9 %copy-start.6 = (f32[64,16]{1,0:T(8,128)S(1)}, f32[64,16]{1,0:T(8,128)}, u32[]{:S(2)}) copy-start(f32[64,16]{1,0:T(8,128)} %copy.97) | copy-start | bytes 12292
